TPU v7x, 32 devices: a whole 2x2x4 slice. The times are simulated.
32 devices in a mesh: dp: 2 (over x), expert: 16 (over z, y, core).
Axes of the slice: x: 2, y: 2, z: 4, core: 2. Of those that a mesh axis runs over, the one named last changes fastest.
Arguments:
- query: bfloat16 [32, 2048], P('dp'), may hold values from -1200 to 1200
- new_kv: bfloat16 [32, 1024], P('dp'), may hold values from -5 to 5
- kv_cache: bfloat16 [32, 256, 1024], P('dp', 'expert'), may hold values from -6 to 6
- lengths: int32 [32], P('dp'), may hold values from 2 to 256, as said below
- fork_parent: int32 [4], replicated, may hold values from 0 to 31, as said below
- fork_child: int32 [4], replicated, may hold values from 0 to 30, as said below
- fork_block: int32 [4], replicated, may hold values from 0 to 15, as said below
- out_weight: bfloat16 [2048, 4096], P('expert'), may hold values from -1 to 1
- residual: bfloat16 [32, 4096], P('dp'), may hold values from -300 to 300
- route_ids: int32 [32, 8], replicated, may hold values from 0 to 15, all different within a row; in each aligned block of 16 rows (0 to 15, 16 to 31, ...) at most 16 rows name the same one
- route_weights: float32 [32, 8], replicated, may hold values from 0.02 to 0.3
- w_gate: bfloat16 [16, 4096, 1024], P('expert', None, 'dp'), may hold values from -0.09375 to 0.09375
- w_up: bfloat16 [16, 4096, 1024], P('expert', None, 'dp'), may hold values from -0.09375 to 0.09375
- w_down: bfloat16 [16, 1024, 4096], P('expert', 'dp'), may hold values from -0.1875 to 0.1875
Outputs:
- attn_proj: bfloat16 [32, 4096], P('dp', 'expert')
- expert_mix: bfloat16 [32, 4096], P('dp', 'expert')
Inputs may be any that keep to these rules, and one draw needn't show every extreme that they name: `lengths`: at least 2; a fork's child has its parent's length. `fork_parent`: fork g * 2 + d takes its parent from the branches g * 16 to (g + 1) * 16 - 1 and its child from d * 16 to (d + 1) * 16 - 1; parents are distinct, children are distinct, and no child is a parent. `fork_child`: see fork_parent. `fork_block`: at most the block that holds the parent's last cached position, (lengths - 1) // 16. `route_ids`: in each aligned block of 16 rows no expert is named by more than 16 rows, a bound that some block reaches.
All inputs are finite; a program needn't handle non-finite values.
Results may differ from a plain program's by a relative error of at most 0.024.
Values may be sent and summed in bfloat16 or wider, within the bound.
A program may use at most 128 MiB of HBM per device.

v0:
```python
import math

import jax
import jax.numpy as jnp
from jax import lax
from jax.sharding import PartitionSpec as P

HD = 128
KVH = 4


def combined_all(array, axis, join):
    gathered = jax.tree.map(
        lambda a, kind: lax.all_gather(a.astype(kind), axis),
        array,
        (jnp.bfloat16, jnp.bfloat16, jnp.bfloat16),
    )

    def take(source):
        return jax.tree.map(
            lambda a, own: lax.dynamic_index_in_dim(a, source, 0, False).astype(own.dtype),
            gathered,
            array,
        )

    return lax.fori_loop(
        1, lax.axis_size(axis), lambda source, state: join(state, take(source)), take(0)
    )


def combine_parts(first, second):
    out_first, peak_first, sum_first = first
    out_second, peak_second, sum_second = second
    highest = jnp.maximum(peak_first, peak_second)
    factor_first = jnp.exp(peak_first - highest)
    factor_second = jnp.exp(peak_second - highest)
    merged_out = out_first * factor_first[..., None] + out_second * factor_second[..., None]
    return (merged_out, highest, sum_first * factor_first + sum_second * factor_second)


def shards(
    query,
    new_kv,
    kv_cache,
    lengths,
    fork_parent,
    fork_child,
    fork_block,
    out_weight,
    residual,
    route_ids,
    route_weights,
    w_gate,
    w_up,
    w_down,
):
    groups = lax.axis_size("dp")
    owners = lax.axis_size("expert")
    group_index = lax.axis_index("dp")
    owner_index = lax.axis_index("expert")
    local_rows = query.shape[0]
    positions_dev = kv_cache.shape[1]
    key_width = KVH * HD
    head_count = query.shape[1] // HD
    grouping = head_count // KVH
    own_heads = head_count // owners
    model_width = residual.shape[1]
    columns = model_width // owners
    outgoing = (
        lax.dynamic_slice_in_dim(fork_parent, group_index * groups, groups)
        - group_index * local_rows
    )
    out_blocks = lax.dynamic_slice_in_dim(fork_block, group_index * groups, groups)
    send_rows = jnp.where(
        (owner_index >= out_blocks)[:, None, None],
        kv_cache[outgoing],
        jnp.zeros((), kv_cache.dtype),
    )
    arrived = lax.all_to_all(send_rows, "dp", split_axis=0, concat_axis=0, tiled=True)
    incoming = jnp.arange(groups, dtype=jnp.int32) * groups + group_index
    targets = fork_child[incoming] - group_index * local_rows
    take_new = owner_index >= fork_block[incoming]
    cache = kv_cache.at[targets].set(jnp.where(take_new[:, None, None], arrived, kv_cache[targets]))
    score_scale = 1.0 / math.sqrt(HD)
    positions = owner_index * positions_dev + jnp.arange(positions_dev, dtype=jnp.int32)
    visible = positions[None, :] < lengths[:, None]
    cached_keys = cache[:, :, :key_width].reshape(local_rows, positions_dev, KVH, HD)
    cached_values = cache[:, :, key_width:].reshape(local_rows, positions_dev, KVH, HD)
    grouped = query.reshape(local_rows, KVH, grouping, HD)
    scores = (
        jnp.einsum("bkgd,bpkd->bkgp", grouped, cached_keys, preferred_element_type=jnp.float32)
        * score_scale
    )
    scores = jnp.where(visible[:, None, None, :], scores, -1e30)
    highest = jnp.max(scores, axis=3)
    weights = jnp.where(visible[:, None, None, :], jnp.exp(scores - highest[..., None]), 0.0)
    weight_sum = jnp.sum(weights, axis=3)
    partial_out = jnp.einsum(
        "bkgp,bpkd->bkgd",
        weights.astype(jnp.bfloat16),
        cached_values,
        preferred_element_type=jnp.float32,
    )
    partial_out = partial_out.reshape(local_rows, head_count, HD)
    highest = highest.reshape(local_rows, head_count)
    weight_sum = weight_sum.reshape(local_rows, head_count)
    merged = combined_all((partial_out, highest, weight_sum), "expert", combine_parts)
    head_out = lax.dynamic_slice_in_dim(merged[0], owner_index * own_heads, own_heads, 1)
    head_peak = lax.dynamic_slice_in_dim(merged[1], owner_index * own_heads, own_heads, 1)
    head_sum = lax.dynamic_slice_in_dim(merged[2], owner_index * own_heads, own_heads, 1)
    own_query = lax.dynamic_slice_in_dim(query, owner_index * own_heads * HD, own_heads * HD, 1)
    own_query = own_query.reshape(local_rows, own_heads, HD).astype(jnp.float32)
    kv_index = (owner_index * own_heads + jnp.arange(own_heads, dtype=jnp.int32)) // grouping
    new_keys = jnp.take(
        new_kv[:, :key_width].reshape(local_rows, KVH, HD), kv_index, axis=1
    ).astype(jnp.float32)
    new_values = jnp.take(
        new_kv[:, key_width:].reshape(local_rows, KVH, HD), kv_index, axis=1
    ).astype(jnp.float32)
    own_score = jnp.sum(own_query * new_keys, axis=2) * score_scale
    new_peak = jnp.maximum(head_peak, own_score)
    old_factor = jnp.exp(head_peak - new_peak)
    own_weight = jnp.exp(own_score - new_peak)
    denominator = head_sum * old_factor + own_weight
    own_rounded = lax.optimization_barrier(own_weight.astype(jnp.bfloat16)).astype(jnp.float32)
    attended = (
        head_out * old_factor[..., None] + own_rounded[..., None] * new_values
    ) / denominator[..., None]
    attended = attended.astype(jnp.bfloat16).reshape(local_rows, own_heads * HD)
    proj_terms = jnp.dot(attended, out_weight, preferred_element_type=jnp.float32)
    projected = lax.psum(proj_terms, "expert")
    stream = residual.astype(jnp.float32) + projected
    inverse = lax.rsqrt(jnp.sum(stream * stream, axis=1, keepdims=True) / model_width + 1e-06)
    normed = (stream * inverse).astype(jnp.bfloat16)
    attn_cols = lax.dynamic_slice_in_dim(projected, owner_index * columns, columns, 1).astype(
        jnp.bfloat16
    )
    top_k = route_ids.shape[1]
    experts_total = w_gate.shape[0] * owners
    capacity = max(2, 2 * local_rows * top_k // experts_total)
    own_ids = lax.dynamic_slice_in_dim(route_ids, group_index * local_rows, local_rows, 0)
    own_gates = lax.dynamic_slice_in_dim(route_weights, group_index * local_rows, local_rows, 0)
    matched = (own_ids == owner_index).astype(jnp.int32).reshape(-1)
    ranking = jnp.cumsum(matched) - 1
    slot_ids = jnp.arange(capacity, dtype=jnp.int32)
    onehot = ((matched[:, None] == 1) & (ranking[:, None] == slot_ids[None, :])).astype(jnp.float32)
    chosen = onehot.reshape(local_rows, top_k, capacity)
    dispatch = jnp.sum(chosen, axis=1).T
    slot_gate = jnp.sum(chosen * own_gates[:, :, None], axis=(0, 1))
    dispatch, slot_gate = (dispatch, slot_gate)
    routed = jnp.dot(
        dispatch.astype(jnp.bfloat16), normed, preferred_element_type=jnp.float32
    ).astype(jnp.bfloat16)
    piece = lax.all_gather(routed, "dp", axis=0, tiled=True)
    gate_proj = jnp.dot(piece, w_gate[0], preferred_element_type=jnp.float32)
    up_proj = jnp.dot(piece, w_up[0], preferred_element_type=jnp.float32)
    hidden = (jax.nn.silu(gate_proj) * up_proj).astype(jnp.bfloat16)
    outputs = jnp.dot(hidden, w_down[0], preferred_element_type=jnp.float32)
    summed = lax.psum_scatter(
        outputs.astype(jnp.bfloat16), "dp", scatter_dimension=0, tiled=True
    ).astype(jnp.float32)
    spread = jnp.dot(dispatch.T * slot_gate[None, :], summed, precision=lax.Precision.HIGHEST)
    mix_cols = lax.psum_scatter(spread, "expert", scatter_dimension=1, tiled=True).astype(
        jnp.bfloat16
    )
    return (attn_cols, mix_cols)


def solution(mesh):
    in_specs = (
        P("dp", None),
        P("dp", None),
        P("dp", "expert", None),
        P("dp"),
        P(),
        P(),
        P(),
        P("expert", None),
        P("dp", None),
        P(),
        P(),
        P("expert", None, "dp"),
        P("expert", None, "dp"),
        P("expert", "dp", None),
    )
    out_specs = (P("dp", "expert"), P("dp", "expert"))
    return jax.shard_map(shards, mesh=mesh, in_specs=in_specs, out_specs=out_specs, check_vma=False)
```

profile of v0, /device:TPU:0, one launch (start us, length us, event | category | flops | bytes accessed | tf_op | source)
XLA Modules:
  0.0 266.3 jit_solution(2027945869942430153)
XLA Ops:
  7.2 1.1 copy.131
  8.3 0.7 compare_select_fusion
  9.1 0.7 dynamic-slice_compare_fusion.1
  9.8 0.5 gather_fusion.2
  10.4 0.7 broadcast_select_fusion
  11.1 4.2 %all-to-all-start = ((bf16[2,16,1024]{2,1,0:T(8,128)(2,1)}), bf16[2,16,1024]{2,1,0:T(8,128)(2,1)S(1)}, u32[]{:S(2)}, u32[]{:S(2)}) async-start(bf16[2,16,1024]{2,1,0:T(8,128)(2,1)} %broadcast_select_fusion), calls=%async_computation | async-start | bytes 131072 | tf_op jit(solution)/shard_map/all_to_all | solution.py:79
  15.3 1.3 gather_fusion.1
  16.6 1.3 gather_fusion
  17.9 0.7 broadcast_compare_fusion
  18.6 0.6 gather_fusion.3
  19.2 0.9 reshape.220
  20.2 0.6 scatter_fusion
  20.9 0.3 fusion.68
  21.2 0.9 convolution_convert_fusion.2
  22.5 0.2 reduce-window.4
  22.7 0.8 fusion.37
  23.7 0.3 fusion.23
  24.3 22.4 %all_gather.17 = bf16[16,16,16]{2,1,0:T(8,128)(2,1)S(1)} all-gather(bf16[1,16,16]{2,1,0:T(8,128)(2,1)S(1)} %copy.83), channel_id=1, replica_groups=mesh['dp'=2,'expert'=16] {'expert'}, dimensions={0}, use_global_device_ids=true | all-gather | bytes 8704 | tf_op jit(solution)/shard_map/all_gather | solution.py:14
  46.8 17.7 %all_gather.16 = bf16[16,16,16]{2,1,0:T(8,128)(2,1)S(1)} all-gather(bf16[1,16,16]{2,1,0:T(8,128)(2,1)S(1)} %copy.81), channel_id=1, replica_groups=mesh['dp'=2,'expert'=16] {'expert'}, dimensions={0}, use_global_device_ids=true | all-gather | bytes 8704 | tf_op jit(solution)/shard_map/all_gather | solution.py:14
  64.5 0.8 fusion.26
  65.3 15.8 %while.20 = (s32[]{:T(128)}, f32[16,16,128]{2,1,0:T(8,128)S(1)}, f32[16,16]{1,0:T(8,128)S(1)}, f32[16,16]{1,0:T(8,128)S(1)}, bf16[16,16,16]{2,1,0:T(8,128)(2,1)S...) while((s32[]{:T(128)}, f32[16,16,128]{2,1,0:T(8,128)S(1)}, ...), condition=%wide.region_4.5_spmd, body=%wide.region_3.4_spmd.sunk | while | flops 133125 | bytes 337047 | solution.py:26
  65.4 1.0 fusion.77
  66.4 1.0 fusion.77
  67.5 1.0 fusion.77
  68.5 1.0 fusion.77
  69.6 1.0 fusion.77
  70.6 1.0 fusion.77
  71.7 1.0 fusion.77
  72.8 1.0 fusion.77
  73.8 1.0 fusion.77
  74.9 1.0 fusion.77
  75.9 1.0 fusion.77
  77.0 1.0 fusion.77
  78.0 1.0 fusion.77
  79.1 1.0 fusion.77
  80.1 1.0 fusion.77
  81.4 1.0 fusion.42
  83.0 87.3 %all-reduce.2.cloned.1.call-done = f32[16,4096]{1,0:T(8,128)} async-done(((f32[16,4096]{1,0:T(8,128)}), f32[16,4096]{1,0:T(8,128)}) %all-reduce.2.cloned.1.call-update) | async-done | bytes 262160 | tf_op jit(solution)/shard_map/psum | solution.py:131
  170.3 1.1 multiply_reduce_fusion
  171.4 1.2 convolution_convert_fusion.1
  172.6 6.6 %all_gather.18 = bf16[32,4096]{1,0:T(8,128)(2,1)S(1)} all-gather(bf16[16,4096]{1,0:T(8,128)(2,1)S(1)} %convolution_convert_fusion.1), channel_id=1, replica_groups=mesh['dp'=2,'expert'=16] {'dp'}, dimensions={0}, use_global_device_ids=true | all-gather | bytes 393216 | tf_op jit(solution)/shard_map/all_gather | solution.py:154
  179.2 3.0 %fusion.6 = f32[32,512]{1,0:T(8,128)S(1)} fusion(bf16[32,4096]{1,0:T(8,128)(2,1)S(1)} %all_gather.18, bf16[1,4096,512]{2,1,0:T(8,128)(2,1)} %param.29), kind=kOutput, calls=%fused_computation.18 | convolution fusion | flops 134217728 | bytes 4521984 | tf_op jit(solution)/shard_map/dot_general | solution.py:155
  182.2 5.8 %convolution_convert_fusion = bf16[32,4096]{1,0:T(8,128)(2,1)} fusion(bf16[1,512,4096]{2,1,0:T(8,128)(2,1)} %param.31, bf16[32,4096]{1,0:T(8,128)(2,1)S(1)} %all_gather.18, bf16[1,4096,512]{2,1,0:T(8,128)(2,1)} %param.30, f32[32,512]{1,0:T(8,128)S(1)} %fusion.6), kind=kOutput, calls=%fused_computation.13 | convolution fusion | flops 268664832 | bytes 8978432 | tf_op jit(solution)/shard_map/dot_general | solution.py:158
  188.0 11.3 %reduce-scatter.3.cloned.1.call-done = bf16[16,4096]{1,0:T(8,128)(2,1)} async-done(((bf16[32,4096]{1,0:T(8,128)(2,1)}), bf16[16,4096]{1,0:T(8,128)(2,1)}) %reduce-scatter.3.cloned.1.call-update) | async-done | bytes 131088 | tf_op jit(solution)/shard_map/reduce_scatter | solution.py:159
  199.3 1.9 fusion.38
  201.2 1.3 dynamic-slice_convert_fusion
  202.5 55.9 %reduce-scatter.5.cloned.1.call-done = f32[16,256]{1,0:T(8,128)} async-done(((f32[16,4096]{1,0:T(8,128)}), f32[16,256]{1,0:T(8,128)}) %reduce-scatter.5.cloned.1.call-update) | async-done | bytes 16400 | tf_op jit(solution)/shard_map/reduce_scatter | solution.py:163
  258.5 1.3 convert_element_type.179
  (70 shorter events, 2.2 us)
Async XLA Ops:
  7.2 74.2 %copy-start = (bf16[128,4096]{1,0:T(8,128)(2,1)S(1)}, bf16[128,4096]{1,0:T(8,128)(2,1)}, u32[]{:S(2)}) copy-start(bf16[128,4096]{1,0:T(8,128)(2,1)} %param.25) | copy-start | bytes 3145732
  7.2 15.0 %copy-start.2 = (bf16[16,1024]{1,0:T(8,128)(2,1)S(1)}, bf16[16,1024]{1,0:T(8,128)(2,1)}, u32[]{:S(2)}) copy-start(bf16[16,1024]{1,0:T(8,128)(2,1)} %param.19) | copy-start | bytes 98308
  7.2 15.1 %copy-start.3 = (s32[32,8]{0,1:T(8,128)S(1)}, s32[32,8]{0,1:T(8,128)}, u32[]{:S(2)}) copy-start(s32[32,8]{0,1:T(8,128)} %param.27) | copy-start | bytes 3076
  11.1 9.0 %all-to-all-start = ((bf16[2,16,1024]{2,1,0:T(8,128)(2,1)}), bf16[2,16,1024]{2,1,0:T(8,128)(2,1)S(1)}, u32[]{:S(2)}, u32[]{:S(2)}) async-start(bf16[2,16,1024]{2,1,0:T(8,128)(2,1)} %broadcast_select_fusion), calls=%async_computation | async-start | bytes 131072 | tf_op jit(solution)/shard_map/all_to_all | solution.py:79
  15.3 49.2 %all-gather.2.cloned.1.call-start = ((), (), s32[]{:S(2)}) async-start(), calls=%async_computation.3 | async-start | bytes 1114112 | tf_op jit(solution)/shard_map/all_gather | solution.py:14
  20.2 62.3 %copy-start.4 = (f32[32,8]{0,1:T(8,128)S(1)}, f32[32,8]{0,1:T(8,128)}, u32[]{:S(2)}) copy-start(f32[32,8]{0,1:T(8,128)} %param.28) | copy-start | bytes 3076
  20.2 150.1 %copy-start.1 = (bf16[16,4096]{1,0:T(8,128)(2,1)S(1)}, bf16[16,4096]{1,0:T(8,128)(2,1)}, u32[]{:S(2)}) copy-start(bf16[16,4096]{1,0:T(8,128)(2,1)} %param.26) | copy-start | bytes 393220
  22.1 148.1 %all-reduce.2.cloned.1.call-start = ((), (), s32[]{:S(2)}) async-start(), calls=%async_computation.4 | async-start | bytes 524288 | tf_op jit(solution)/shard_map/psum | solution.py:131
  82.5 116.9 %reduce-scatter.3.cloned.1.call-start = ((), (), s32[]{:S(2)}) async-start(), calls=%async_computation.5 | async-start | bytes 393216 | tf_op jit(solution)/shard_map/reduce_scatter | solution.py:159
  188.0 70.5 %reduce-scatter.5.cloned.1.call-start = ((), (), s32[]{:S(2)}) async-start(), calls=%async_computation.6 | async-start | bytes 278528 | tf_op jit(solution)/shard_map/reduce_scatter | solution.py:163
Sparse Core Ops, SparseCore 0:
  22.3 40.3 all-gather.1
  82.6 87.6 all-reduce.1
  188.1 11.1 reduce-scatter.2
  203.1 55.3 reduce-scatter.4
where the time goes:
time: 268 us; the launch traced here: 266 us
  waiting for transfers between devices  155 us (58%)
  blocking collectives  46.8 us (17%)
  other arithmetic  23.3 us (9%)
  matrix products  14.1 us (5%)
  between operations  14 us (5%)
  local copies, waits for them, and re-layouts  8.79 us (3%)
  starting transfers between devices  4.33 us (2%)
    psum x1, waiting for transfers between devices, shards(): projected = lax.psum(proj_terms, 'expert')  87.3 us
    reduce_scatter x1, waiting for transfers between devices, shards(): lax.psum_scatter(spread, 'expert', scatter_dimension=1, tiled=True)  55.9 us
    all_gather x2, blocking collectives, combined_all(): lax.all_gather(a.astype(kind), axis)  40.1 us
    add x15, other arithmetic, combine_parts(): out_first * factor_first[..., None] + out_second * factor_second[..., None]  15 us
    reduce_scatter x1, waiting for transfers between devices, shards(): lax.psum_scatter(outputs.astype(jnp.bfloat16), 'dp', scatter_dimension=0,...  11.3 us
    all_gather x1, blocking collectives, shards(): piece = lax.all_gather(routed, 'dp', axis=0, tiled=True)  6.61 us
    dot_general x1, matrix products, shards(): outputs = jnp.dot(hidden, w_down[0], preferred_element_type=jnp.float32)  5.81 us
  transfers between devices with their start and end apart: 5, of which 3 were waited for; matrix products, arithmetic and copies ran while one was open for 3% of the time, Pallas kernels for 0%

commit v1 on v0

v1 whole, which is shorter than its diff:
```python
import functools
import math

import jax
import jax.numpy as jnp
from jax import lax
from jax.experimental import pallas as pl
from jax.experimental.pallas import tpu as pltpu
from jax.sharding import PartitionSpec as P

HD = 128
KVH = 4
MESH = pl.DeviceIdType.MESH
F32 = jnp.float32
BF16 = jnp.bfloat16
HIDDEN_SCORE = -1e30


def layer(
    groups,
    owners,
    slice_residual,
    lengths,
    fork_parent,
    fork_child,
    fork_block,
    query,
    new_kv,
    kv_cache,
    residual,
    route_ids,
    route_weights,
    out_weight,
    w_gate,
    w_up,
    w_down,
    attn_out,
    mix_out,
    cache,
    out_held,
    gate_held,
    up_held,
    down_held,
    fork_send,
    fork_recv,
    part_send,
    part_recv,
    proj_send,
    proj_recv,
    stream,
    mix_send,
    mix_recv,
    load_sem,
    fork_send_sem,
    fork_recv_sem,
    part_sem,
    proj_sem,
    stream_send_sem,
    stream_recv_sem,
    mix_sem,
):
    group = lax.axis_index("dp")
    owner = lax.axis_index("expert")
    devices = groups * owners
    rows = query.shape[0]
    positions_dev = kv_cache.shape[1]
    key_width = KVH * HD
    grouping = query.shape[1] // HD // KVH
    width = w_gate.shape[1]
    columns = width // owners
    fork_groups = math.isqrt(fork_parent.shape[0])
    held_groups = fork_groups // groups
    pairs = [(i, k) for i in range(held_groups) for k in range(held_groups)]

    barrier = pltpu.get_barrier_semaphore()

    def greet(step, carry):
        place = lax.rem(group * owners + owner + step, devices)
        pl.semaphore_signal(
            barrier,
            inc=1,
            device_id=(place // owners, lax.rem(place, owners)),
            device_id_type=MESH,
        )
        return carry

    lax.fori_loop(1, devices, greet, 0)

    loads = [
        pltpu.make_async_copy(out_weight, out_held, load_sem.at[0]),
        pltpu.make_async_copy(w_gate.at[0], gate_held, load_sem.at[1]),
        pltpu.make_async_copy(w_up.at[0], up_held, load_sem.at[2]),
        pltpu.make_async_copy(w_down.at[0], down_held, load_sem.at[3]),
    ]
    for load in loads:
        load.start()

    def send(source, target, send_sem, recv_sem, to_group, to_owner):
        pltpu.make_async_remote_copy(
            src_ref=source,
            dst_ref=target,
            send_sem=send_sem,
            recv_sem=recv_sem,
            device_id=(to_group, to_owner),
            device_id_type=MESH,
        ).start()

    def take(ref, sem):
        pltpu.make_async_copy(ref, ref, sem).wait()

    def fork_index(parent_group, child_group, pair):
        return (parent_group * held_groups + pair[0]) * fork_groups + (
            child_group * held_groups + pair[1]
        )

    for away in range(groups):
        target = lax.rem(group + away, groups)
        for slot, pair in enumerate(pairs):
            parent = lax.rem(fork_parent[fork_index(group, target, pair)], rows)
            chosen = kv_cache[parent]
            if away == 0:
                fork_recv[0, slot] = chosen
            else:
                fork_send[away, slot] = chosen
    pl.semaphore_wait(barrier, devices - 1)
    for away in range(1, groups):
        target = lax.rem(group + away, groups)
        send(
            fork_send.at[away],
            fork_recv.at[away],
            fork_send_sem.at[away],
            fork_recv_sem.at[away],
            target,
            owner,
        )

    shape = (rows, rows * positions_dev)
    row_at = lax.broadcasted_iota(jnp.int32, shape, 0)
    column_at = lax.broadcasted_iota(jnp.int32, shape, 1)
    length_at = jnp.zeros(shape, jnp.int32)
    for b in range(rows):
        length_at = jnp.where(row_at == b, lengths[b], length_at)
    position_at = owner * positions_dev + lax.rem(column_at, positions_dev)
    seen = (column_at // positions_dev == row_at) & (position_at < length_at)
    bias = jnp.where(seen, 0.0, HIDDEN_SCORE).astype(F32)
    bias = jnp.concatenate([bias] * grouping, axis=0)
    score_scale = 1.0 / math.sqrt(HD)
    own_query = query[:, pl.ds(pl.multiple_of(owner * HD, HD), HD)].astype(F32)
    own_kv = owner // grouping
    new_key = new_kv[:, pl.ds(pl.multiple_of(own_kv * HD, HD), HD)].astype(F32)
    new_value = new_kv[:, pl.ds(pl.multiple_of(key_width + own_kv * HD, HD), HD)].astype(F32)
    own_score = jnp.sum(own_query * new_key, axis=1, keepdims=True) * score_scale

    for away in range(1, groups):
        take(fork_recv.at[away], fork_recv_sem.at[away])
    for b in range(rows):
        kept = kv_cache[b].astype(F32)
        for away in range(groups):
            source = lax.rem(group + groups - away, groups)
            for slot, pair in enumerate(pairs):
                fork = fork_index(source, group, pair)
                hit = (fork_child[fork] - group * rows == b) & (owner >= fork_block[fork])
                kept = jnp.where(hit, fork_recv[away, slot].astype(F32), kept)
        cache[b] = kept.astype(BF16)

    lane = lax.broadcasted_iota(jnp.int32, (grouping * rows, HD), 1)
    for j in range(KVH):
        heads = [j * grouping + i for i in range(grouping)]
        grouped = jnp.concatenate([query[:, h * HD : (h + 1) * HD] for h in heads], axis=0)
        keys = cache[:, :, j * HD : (j + 1) * HD].reshape(rows * positions_dev, HD)
        values = cache[:, :, key_width + j * HD : key_width + (j + 1) * HD].reshape(
            rows * positions_dev, HD
        )
        scores = lax.dot_general(
            grouped, keys, (((1,), (1,)), ((), ())), preferred_element_type=F32
        )
        scores = scores * score_scale + bias
        peak = jnp.max(scores, axis=1, keepdims=True)
        weights = jnp.where(scores > 0.5 * HIDDEN_SCORE, jnp.exp(scores - peak), 0.0)
        total = jnp.sum(weights, axis=1, keepdims=True)
        part = jnp.dot(weights.astype(BF16), values, preferred_element_type=F32)
        peak_high = peak.astype(BF16).astype(F32)
        peak_mid = (peak - peak_high).astype(BF16).astype(F32)
        peak_low = peak - peak_high - peak_mid
        total_high = total.astype(BF16).astype(F32)
        total_low = total - total_high
        stats = jnp.where(lane == 0, peak_high, 0.0)
        stats = jnp.where(lane == 1, peak_mid, stats)
        stats = jnp.where(lane == 2, peak_low, stats)
        stats = jnp.where(lane == 3, total_high, stats)
        stats = jnp.where(lane == 4, total_low, stats)
        message = jnp.concatenate([part, stats], axis=1).astype(BF16)
        for i, h in enumerate(heads):
            part_send[h] = message[i * rows : (i + 1) * rows]

    def send_part(step, carry):
        target = lax.rem(owner + step, owners)
        send(
            part_send.at[target], part_recv.at[owner], part_sem.at[0], part_sem.at[1], group, target
        )
        return carry

    lax.fori_loop(1, owners, send_part, 0)
    part_recv[owner] = part_send[owner]
    picked = lax.broadcasted_iota(jnp.int32, (HD, 2 * HD), 0)
    side = lax.broadcasted_iota(jnp.int32, (HD, 2 * HD), 1) // HD
    spread = ((side == 0) & (picked < 3)) | ((side == 1) & ((picked == 3) | (picked == 4)))
    spread = jnp.where(spread, 1.0, 0.0).astype(BF16)
    take(part_recv.at[pl.ds(0, owners - 1)], part_sem.at[1])

    stats = part_recv[:, :, HD:].reshape(owners * rows, HD)
    stats = jnp.dot(stats, spread, preferred_element_type=F32).reshape(owners, rows, 2 * HD)
    peaks, totals = stats[:, :, :HD], stats[:, :, HD:]
    highest = jnp.maximum(jnp.max(peaks, axis=0), own_score)
    factors = jnp.exp(peaks - highest[None])
    own_weight = jnp.exp(own_score - highest)
    denominator = jnp.sum(totals * factors, axis=0) + own_weight
    attended = jnp.sum(part_recv[:, :, :HD].astype(F32) * factors, axis=0)
    attended = attended + own_weight.astype(BF16).astype(F32) * new_value
    attended = (attended / denominator).astype(BF16)

    loads[0].wait()
    tile = max(columns, 1024)
    blocks = tile // columns
    for k in range(width // tile):
        terms = jnp.dot(
            attended, out_held[:, k * tile : (k + 1) * tile], preferred_element_type=F32
        ).astype(BF16)
        for i in range(blocks):
            proj_send[k * blocks + i] = terms[:, i * columns : (i + 1) * columns]

    def send_proj(step, carry):
        target = lax.rem(owner + step, owners)
        send(
            proj_send.at[target], proj_recv.at[owner], proj_sem.at[0], proj_sem.at[1], group, target
        )
        return carry

    lax.fori_loop(1, owners, send_proj, 0)
    proj_recv[owner] = proj_send[owner]
    if slice_residual:
        start = pl.multiple_of(owner * columns, 128)
        own_residual = residual[:, pl.ds(start, columns)].astype(F32)
    else:
        own_residual = residual[...].astype(F32)
    take(proj_recv.at[pl.ds(0, owners - 1)], proj_sem.at[1])
    projected = jnp.sum(proj_recv[...].astype(F32), axis=0)
    attn_out[...] = projected.astype(BF16)
    own_rows = pl.ds(pl.multiple_of(group * rows, rows), rows)
    stream[owner, own_rows, :] = (own_residual + projected).astype(BF16)

    def send_stream(step, carry):
        target = lax.rem(owner + step, owners)
        for away in range(groups):
            to_group = lax.rem(group + away, groups)

            def go():
                send(
                    stream.at[owner, own_rows],
                    stream.at[owner, own_rows],
                    stream_send_sem,
                    stream_recv_sem.at[owner, group],
                    to_group,
                    target,
                )

            if away == 0:
                pl.when(step > 0)(go)
            else:
                go()
        return carry

    lax.fori_loop(0, owners, send_stream, 0)
    tokens = groups * rows
    lane_ids = route_ids[...]
    gates = jnp.sum(
        jnp.where(lane_ids == owner, route_weights[...], 0.0), axis=1, keepdims=True
    )
    loads[1].wait()
    loads[2].wait()
    inner = tile // columns
    units = gate_held.shape[1]

    def expand(step, state):
        gate_sum, up_sum, squares = state
        chunk = lax.rem(owner // inner + step, owners // inner)
        for i in range(inner):
            source = chunk * inner + i
            for g in range(groups):

                @pl.when((source != owner) | (g != group))
                def _():
                    take(
                        stream.at[source, pl.ds(g * rows, rows)], stream_recv_sem.at[source, g]
                    )

        x = jnp.concatenate([stream[chunk * inner + i] for i in range(inner)], axis=1)
        depth = pl.ds(pl.multiple_of(chunk * tile, tile), tile)
        gate_sum = gate_sum + jnp.dot(x, gate_held[depth, :], preferred_element_type=F32)
        up_sum = up_sum + jnp.dot(x, up_held[depth, :], preferred_element_type=F32)
        wide = x.astype(F32)
        return gate_sum, up_sum, squares + jnp.sum(wide * wide, axis=1, keepdims=True)

    zero = jnp.zeros((tokens, units), F32)
    gate_sum, up_sum, squares = lax.fori_loop(
        0, owners // inner, expand, (zero, zero, jnp.zeros((tokens, 1), F32))
    )
    inverse = lax.rsqrt(squares / width + 1e-06)
    gate_sum = gate_sum * inverse
    hidden = (gate_sum / (1.0 + jnp.exp(-gate_sum)) * (up_sum * inverse)).astype(BF16)

    loads[3].wait()
    place = group * owners + owner

    def contract(step, carry):
        chunk = lax.rem(owner // inner + step, owners // inner)
        span = pl.ds(pl.multiple_of(chunk * tile, tile), tile)
        terms = jnp.dot(hidden, down_held[:, span], preferred_element_type=F32)
        terms = (terms * gates).astype(BF16)
        for i in range(inner):
            target = chunk * inner + i
            for g in range(groups):
                slot = g * owners + target
                mix_send[slot] = terms[g * rows : (g + 1) * rows, i * columns : (i + 1) * columns]

                @pl.when(slot != place)
                def _():
                    send(
                        mix_send.at[slot],
                        mix_recv.at[place],
                        mix_sem.at[0],
                        mix_sem.at[1],
                        g,
                        target,
                    )

        return carry

    lax.fori_loop(0, owners // inner, contract, 0)
    mix_recv[place] = mix_send[place]
    take(mix_recv.at[pl.ds(0, devices - 1)], mix_sem.at[1])
    mix_out[...] = jnp.sum(mix_recv[...].astype(F32), axis=0).astype(BF16)

    for away in range(1, groups):
        take(fork_send.at[away], fork_send_sem.at[away])
    take(part_send.at[pl.ds(0, owners - 1)], part_sem.at[0])
    take(proj_send.at[pl.ds(0, owners - 1)], proj_sem.at[0])
    take(mix_send.at[pl.ds(0, devices - 1)], stream_send_sem)
    take(mix_send.at[pl.ds(0, devices - 1)], mix_sem.at[0])


def shards(
    query,
    new_kv,
    kv_cache,
    lengths,
    fork_parent,
    fork_child,
    fork_block,
    out_weight,
    residual,
    route_ids,
    route_weights,
    w_gate,
    w_up,
    w_down,
):
    groups = lax.axis_size("dp")
    owners = lax.axis_size("expert")
    devices = groups * owners
    rows, positions_dev, _ = kv_cache.shape
    heads = query.shape[1] // HD
    width = residual.shape[1]
    columns = width // owners
    slice_residual = columns % 128 == 0
    if not slice_residual:
        residual = lax.dynamic_slice_in_dim(
            residual, lax.axis_index("expert") * columns, columns, 1
        )
    fork_rows = (math.isqrt(fork_parent.shape[0]) // groups) ** 2
    fork_shape = (groups, fork_rows) + kv_cache.shape[1:]
    smem = pl.BlockSpec(memory_space=pltpu.SMEM)
    vmem = pl.BlockSpec(memory_space=pltpu.VMEM)
    anywhere = pl.BlockSpec(memory_space=pl.ANY)
    dma = pltpu.SemaphoreType.DMA
    block = jax.ShapeDtypeStruct((rows, columns), BF16)
    return pl.pallas_call(
        functools.partial(layer, groups, owners, slice_residual),
        out_shape=(block, block),
        in_specs=[smem] * 4 + [vmem] * 6 + [anywhere] * 4,
        out_specs=(vmem, vmem),
        scratch_shapes=[
            pltpu.VMEM(kv_cache.shape, BF16),
            pltpu.VMEM(out_weight.shape, BF16),
            pltpu.VMEM(w_gate.shape[1:], BF16),
            pltpu.VMEM(w_up.shape[1:], BF16),
            pltpu.VMEM(w_down.shape[1:], BF16),
            pltpu.VMEM(fork_shape, BF16),
            pltpu.VMEM(fork_shape, BF16),
            pltpu.VMEM((heads, rows, 2 * HD), BF16),
            pltpu.VMEM((owners, rows, 2 * HD), BF16),
            pltpu.VMEM((owners, rows, columns), BF16),
            pltpu.VMEM((owners, rows, columns), BF16),
            pltpu.VMEM((owners, groups * rows, columns), BF16),
            pltpu.VMEM((devices, rows, columns), BF16),
            pltpu.VMEM((devices, rows, columns), BF16),
            dma((4,)),
            dma((groups,)),
            dma((groups,)),
            dma((2,)),
            dma((2,)),
            dma,
            dma((owners, groups)),
            dma((2,)),
        ],
        compiler_params=pltpu.CompilerParams(
            collective_id=0, has_side_effects=True, vmem_limit_bytes=48 * 1024 * 1024
        ),
    )(
        lengths,
        fork_parent,
        fork_child,
        fork_block,
        query,
        new_kv,
        kv_cache,
        residual,
        route_ids,
        route_weights,
        out_weight,
        w_gate,
        w_up,
        w_down,
    )


def solution(mesh):
    in_specs = (
        P("dp", None),
        P("dp", None),
        P("dp", "expert", None),
        P("dp"),
        P(),
        P(),
        P(),
        P("expert", None),
        P("dp", None),
        P(),
        P(),
        P("expert", None, "dp"),
        P("expert", None, "dp"),
        P("expert", "dp", None),
    )
    out_specs = (P("dp", "expert"), P("dp", "expert"))
    return jax.shard_map(shards, mesh=mesh, in_specs=in_specs, out_specs=out_specs, check_vma=False)
```

time: 268 us -> 50.9 us (0.19)
  waiting for transfers between devices: 155 us -> 0 us
  blocking collectives: 46.8 us -> 0 us
  Pallas kernels: 0 us -> 37.2 us
  other arithmetic: 23.3 us -> 0 us
  matrix products: 14.1 us -> 0 us
  between operations: 14 us -> 0.65 us
  starting transfers between devices: 4.33 us -> 0 us
  local copies, waits for them, and re-layouts: 8.79 us -> 12.3 us
    psum x1 -> x0, waiting for transfers between devices: 87.3 us -> none  [shards(): projected = lax.psum(proj_terms, 'expert')]
    reduce_scatter x2 -> x0, waiting for transfers between devices: 67.2 us -> none  [the longest x1 55.9 us: shards(): lax.psum_scatter(spread, 'expert', scatter_dimension=1, tiled=True)]
    all_gather x3 -> x0, blocking collectives: 46.8 us -> none  [the longest x2 40.1 us: combined_all(): lax.all_gather(a.astype(kind), axis)]
    pallas_call x0 -> x1, Pallas kernels: none -> 37.2 us  [shards(): pl.pallas_call(functools.partial(layer, groups, owners, slice_residual),...]
    add x31 -> x0, other arithmetic: 15.3 us -> none  [the longest x15 15 us: combine_parts(): out_first * factor_first[..., None] + out_second * factor_second[..., None]]
    dot_general x7 -> x0, matrix products: 14.1 us -> none  [the longest x1 5.81 us: shards(): outputs = jnp.dot(hidden, w_down[0], preferred_element_type=jnp.float32)]
    unnamed x12 -> x24, local copies, waits for them, and re-layouts: 1.21 us -> 12.3 us
    all_to_all x1 -> x0, starting transfers between devices: 4.21 us -> none  [shards(): lax.all_to_all(send_rows, 'dp', split_axis=0, concat_axis=0, tiled=True)]
  transfers between devices with their start and end apart: 5 -> 0, of which waited for: 3 -> 0; matrix products, arithmetic and copies ran while one was open for 3% -> 0% of each run, Pallas kernels for 0% -> 0%
where the time goes in v1:
time: 50.9 us; the launch traced here: 50.2 us
  Pallas kernels  37.2 us (73%)
  local copies, waits for them, and re-layouts  12.3 us (24%)
  between operations  0.65 us (1%)
    pallas_call x1, Pallas kernels, shards(): pl.pallas_call(functools.partial(layer, groups, owners, slice_residual),...  37.2 us
    unnamed x24, local copies, waits for them, and re-layouts  12.3 us

profile of v1, /device:TPU:0, one launch (start us, length us, event | category | flops | bytes accessed | tf_op | source)
XLA Modules:
  0.0 50.2 jit_solution(12911164136926367094)
XLA Ops:
  0.6 0.8 %copy.16.route_ids = s32[32,8]{1,0:T(8,128)S(1)} copy(s32[32,8]{0,1:T(8,128)} %param.23) | data formatting | bytes 2048 | tf_op args[9]
  1.4 0.8 %copy.17.route_weights = f32[32,8]{1,0:T(8,128)S(1)} copy(f32[32,8]{0,1:T(8,128)} %param.24) | data formatting | bytes 2048 | tf_op args[10]
  2.2 0.0 copy-start
  2.2 2.2 %copy-done = bf16[1,4096,512]{2,1,0:T(8,128)(2,1)S(1)} copy-done((bf16[1,4096,512]{2,1,0:T(8,128)(2,1)S(1)}, bf16[1,4096,512]{2,1,0:T(8,128)(2,1)}, u32[]{:S(2)}) %copy-start) | copy-done | bytes 4194328
  4.3 0.0 copy-start.1
  4.3 1.2 %copy-done.1 = bf16[128,4096]{1,0:T(8,128)(2,1)S(1)} copy-done((bf16[128,4096]{1,0:T(8,128)(2,1)S(1)}, bf16[128,4096]{1,0:T(8,128)(2,1)}, u32[]{:S(2)}) %copy-start.1) | copy-done | bytes 1048600
  5.6 0.0 copy-start.2
  5.6 1.0 %copy-done.2 = bf16[16,16,1024]{2,1,0:T(8,128)(2,1)S(1)} copy-done((bf16[16,16,1024]{2,1,0:T(8,128)(2,1)S(1)}, bf16[16,16,1024]{2,1,0:T(8,128)(2,1)}, u32[]{:S(2)}) %copy-start.2) | copy-done | bytes 524312
  6.6 0.0 copy-start.3
  6.6 0.9 %copy-done.3 = bf16[16,4096]{1,0:T(8,128)(2,1)S(1)} copy-done((bf16[16,4096]{1,0:T(8,128)(2,1)S(1)}, bf16[16,4096]{1,0:T(8,128)(2,1)}, u32[]{:S(2)}) %copy-start.3) | copy-done | bytes 131096
  7.5 0.0 copy-start.4
  7.5 0.8 %copy-done.4 = bf16[16,2048]{1,0:T(8,128)(2,1)S(1)} copy-done((bf16[16,2048]{1,0:T(8,128)(2,1)S(1)}, bf16[16,2048]{1,0:T(8,128)(2,1)}, u32[]{:S(2)}) %copy-start.4) | copy-done | bytes 65560
  8.4 0.0 copy-start.5
  8.4 0.8 %copy-done.5 = bf16[16,1024]{1,0:T(8,128)(2,1)S(1)} copy-done((bf16[16,1024]{1,0:T(8,128)(2,1)S(1)}, bf16[16,1024]{1,0:T(8,128)(2,1)}, u32[]{:S(2)}) %copy-start.5) | copy-done | bytes 32792
  9.1 0.0 copy-start.6
  9.1 0.7 %copy-done.6 = s32[16]{0:T(128)S(1)} copy-done((s32[16]{0:T(128)S(1)}, s32[16]{0:T(128)}, u32[]{:S(2)}) %copy-start.6) | copy-done | bytes 88
  9.8 0.0 copy-start.7
  9.8 0.7 %copy-done.7 = s32[4]{0:T(128)S(1)} copy-done((s32[4]{0:T(128)S(1)}, s32[4]{0:T(128)}, u32[]{:S(2)}) %copy-start.7) | copy-done | bytes 40
  10.4 0.0 copy-start.8
  10.4 0.7 %copy-done.8 = s32[4]{0:T(128)S(1)} copy-done((s32[4]{0:T(128)S(1)}, s32[4]{0:T(128)}, u32[]{:S(2)}) %copy-start.8) | copy-done | bytes 40
  11.1 0.0 copy-start.9
  11.1 0.7 %copy-done.9 = s32[4]{0:T(128)S(1)} copy-done((s32[4]{0:T(128)S(1)}, s32[4]{0:T(128)}, u32[]{:S(2)}) %copy-start.9) | copy-done | bytes 40
  11.7 37.2 %shard_map.149 = (bf16[16,256]{1,0:T(8,128)(2,1)S(1)}, bf16[16,256]{1,0:T(8,128)(2,1)S(1)}) custom-call(s32[16]{0:T(128)S(1)} %copy-done.6, s32[4]{0:T(128)S(1)} %copy-done.7, s32[4]{0:T(128)S(1)} %copy-done.8, s32[4]{0:T(128)S(1)} %copy-done.9, bf16[16,2048]{1,0:T(8,128)(2,1)S(1)} %copy-done.4, bf16[16,1024]{1,0:T(8,128)(2,1)S(1)} %copy-done.5, ...), custom_call_target="tpu_custom_call" | custom-call | tf_op jit(solution)/shard_map/pallas_call | solution.py:387
  49.0 0.6 %copy.20 = bf16[16,256]{1,0:T(8,128)(2,1)} copy(bf16[16,256]{1,0:T(8,128)(2,1)S(1)} %get-tuple-element.4) | data formatting | bytes 16384
  49.6 0.6 %copy.21 = bf16[16,256]{1,0:T(8,128)(2,1)} copy(bf16[16,256]{1,0:T(8,128)(2,1)S(1)} %get-tuple-element.5) | data formatting | bytes 16384
Async XLA Ops:
  2.2 2.2 %copy-start = (bf16[1,4096,512]{2,1,0:T(8,128)(2,1)S(1)}, bf16[1,4096,512]{2,1,0:T(8,128)(2,1)}, u32[]{:S(2)}) copy-start(bf16[1,4096,512]{2,1,0:T(8,128)(2,1)} %w_gate.1) | copy-start | bytes 12582916
  4.3 1.2 %copy-start.1 = (bf16[128,4096]{1,0:T(8,128)(2,1)S(1)}, bf16[128,4096]{1,0:T(8,128)(2,1)}, u32[]{:S(2)}) copy-start(bf16[128,4096]{1,0:T(8,128)(2,1)} %out_weight.1) | copy-start | bytes 3145732
  5.6 1.0 %copy-start.2 = (bf16[16,16,1024]{2,1,0:T(8,128)(2,1)S(1)}, bf16[16,16,1024]{2,1,0:T(8,128)(2,1)}, u32[]{:S(2)}) copy-start(bf16[16,16,1024]{2,1,0:T(8,128)(2,1)} %kv_cache.1) | copy-start | bytes 1572868
  6.6 0.9 %copy-start.3 = (bf16[16,4096]{1,0:T(8,128)(2,1)S(1)}, bf16[16,4096]{1,0:T(8,128)(2,1)}, u32[]{:S(2)}) copy-start(bf16[16,4096]{1,0:T(8,128)(2,1)} %residual.1) | copy-start | bytes 393220
  7.5 0.8 %copy-start.4 = (bf16[16,2048]{1,0:T(8,128)(2,1)S(1)}, bf16[16,2048]{1,0:T(8,128)(2,1)}, u32[]{:S(2)}) copy-start(bf16[16,2048]{1,0:T(8,128)(2,1)} %query.1) | copy-start | bytes 196612
  8.4 0.8 %copy-start.5 = (bf16[16,1024]{1,0:T(8,128)(2,1)S(1)}, bf16[16,1024]{1,0:T(8,128)(2,1)}, u32[]{:S(2)}) copy-start(bf16[16,1024]{1,0:T(8,128)(2,1)} %new_kv.1) | copy-start | bytes 98308
  9.1 0.7 %copy-start.6 = (s32[16]{0:T(128)S(1)}, s32[16]{0:T(128)}, u32[]{:S(2)}) copy-start(s32[16]{0:T(128)} %lengths.1) | copy-start | bytes 196
  9.8 0.7 %copy-start.7 = (s32[4]{0:T(128)S(1)}, s32[4]{0:T(128)}, u32[]{:S(2)}) copy-start(s32[4]{0:T(128)} %fork_parent.1) | copy-start | bytes 52
  10.4 0.7 %copy-start.8 = (s32[4]{0:T(128)S(1)}, s32[4]{0:T(128)}, u32[]{:S(2)}) copy-start(s32[4]{0:T(128)} %fork_child.1) | copy-start | bytes 52
  11.1 0.7 %copy-start.9 = (s32[4]{0:T(128)S(1)}, s32[4]{0:T(128)}, u32[]{:S(2)}) copy-start(s32[4]{0:T(128)} %fork_block.1) | copy-start | bytes 52

commit v2 on v1

--- a/solution.py
+++ b/solution.py
@@ -20,6 +20,22 @@
     groups,
     owners,
     slice_residual,
+    lengths_in,
+    fork_parent_in,
+    fork_child_in,
+    fork_block_in,
+    query_in,
+    new_kv_in,
+    kv_cache_in,
+    residual_in,
+    route_ids_in,
+    route_weights_in,
+    out_weight,
+    w_gate,
+    w_up,
+    w_down,
+    attn_out,
+    mix_out,
     lengths,
     fork_parent,
     fork_child,
@@ -30,13 +46,6 @@
     residual,
     route_ids,
     route_weights,
-    out_weight,
-    w_gate,
-    w_up,
-    w_down,
-    attn_out,
-    mix_out,
-    cache,
     out_held,
     gate_held,
     up_held,
@@ -51,6 +60,7 @@
     mix_send,
     mix_recv,
     load_sem,
+    small_sem,
     fork_send_sem,
     fork_recv_sem,
     part_sem,
@@ -84,6 +94,27 @@
         )
         return carry
 
+    start = pl.multiple_of(owner * columns, columns)
+    wanted = residual_in.at[:, pl.ds(start, columns)] if slice_residual else residual_in
+    small = [
+        pltpu.make_async_copy(source, held, small_sem.at[i])
+        for i, (source, held) in enumerate(
+            [
+                (fork_parent_in, fork_parent),
+                (kv_cache_in, kv_cache),
+                (fork_child_in, fork_child),
+                (fork_block_in, fork_block),
+                (lengths_in, lengths),
+                (query_in, query),
+                (new_kv_in, new_kv),
+                (wanted, residual),
+                (route_ids_in, route_ids),
+                (route_weights_in, route_weights),
+            ]
+        )
+    ]
+    for load in small:
+        load.start()
     lax.fori_loop(1, devices, greet, 0)
 
     loads = [
@@ -113,6 +144,8 @@
             child_group * held_groups + pair[1]
         )
 
+    small[0].wait()
+    small[1].wait()
     for away in range(groups):
         target = lax.rem(group + away, groups)
         for slot, pair in enumerate(pairs):
@@ -122,6 +155,40 @@
                 fork_recv[0, slot] = chosen
             else:
                 fork_send[away, slot] = chosen
+    for load in small[2:7]:
+        load.wait()
+
+    def row_lengths(shape):
+        row_at = lax.broadcasted_iota(jnp.int32, shape, 0)
+        length_at = jnp.zeros(shape, jnp.int32)
+        for b in range(rows):
+            length_at = jnp.where(row_at == b, lengths[b], length_at)
+        column_at = lax.broadcasted_iota(jnp.int32, shape, 1)
+        position_at = owner * positions_dev + lax.rem(column_at, positions_dev)
+        return row_at, column_at // positions_dev, position_at < length_at
+
+    def bias_of(seen):
+        bias = jnp.where(seen, 0.0, HIDDEN_SCORE).astype(F32)
+        return jnp.concatenate([bias] * grouping, axis=0)
+
+    children = []
+    for away in range(groups):
+        source = lax.rem(group + groups - away, groups)
+        for pair in pairs:
+            fork = fork_index(source, group, pair)
+            child = fork_child[fork] - group * rows
+            children.append(jnp.where(owner >= fork_block[fork], child, -1))
+    row_at, branch_at, seen = row_lengths((rows, rows * positions_dev))
+    seen = seen & (branch_at == row_at)
+    for child in children:
+        seen = seen & (row_at != child)
+    bias = bias_of(seen)
+    row_at, fork_at, seen = row_lengths((rows, len(children) * positions_dev))
+    child_at = jnp.full(row_at.shape, -1, jnp.int32)
+    for i, child in enumerate(children):
+        child_at = jnp.where(fork_at == i, child, child_at)
+    fork_bias = bias_of(seen & (child_at == row_at))
+
     pl.semaphore_wait(barrier, devices - 1)
     for away in range(1, groups):
         target = lax.rem(group + away, groups)
@@ -134,51 +201,46 @@
             owner,
         )
 
-    shape = (rows, rows * positions_dev)
-    row_at = lax.broadcasted_iota(jnp.int32, shape, 0)
-    column_at = lax.broadcasted_iota(jnp.int32, shape, 1)
-    length_at = jnp.zeros(shape, jnp.int32)
-    for b in range(rows):
-        length_at = jnp.where(row_at == b, lengths[b], length_at)
-    position_at = owner * positions_dev + lax.rem(column_at, positions_dev)
-    seen = (column_at // positions_dev == row_at) & (position_at < length_at)
-    bias = jnp.where(seen, 0.0, HIDDEN_SCORE).astype(F32)
-    bias = jnp.concatenate([bias] * grouping, axis=0)
     score_scale = 1.0 / math.sqrt(HD)
+
+    def raw_scores(j, keys):
+        heads = [j * grouping + i for i in range(grouping)]
+        grouped = jnp.concatenate([query[:, h * HD : (h + 1) * HD] for h in heads], axis=0)
+        scores = lax.dot_general(
+            grouped, keys, (((1,), (1,)), ((), ())), preferred_element_type=F32
+        )
+        return scores * score_scale
+
+    def head_rows(ref, at):
+        return ref[..., at : at + HD].reshape(-1, HD)
+
+    own_scores = [raw_scores(j, head_rows(kv_cache, j * HD)) + bias for j in range(KVH)]
     own_query = query[:, pl.ds(pl.multiple_of(owner * HD, HD), HD)].astype(F32)
     own_kv = owner // grouping
     new_key = new_kv[:, pl.ds(pl.multiple_of(own_kv * HD, HD), HD)].astype(F32)
     new_value = new_kv[:, pl.ds(pl.multiple_of(key_width + own_kv * HD, HD), HD)].astype(F32)
     own_score = jnp.sum(own_query * new_key, axis=1, keepdims=True) * score_scale
-
     for away in range(1, groups):
         take(fork_recv.at[away], fork_recv_sem.at[away])
-    for b in range(rows):
-        kept = kv_cache[b].astype(F32)
-        for away in range(groups):
-            source = lax.rem(group + groups - away, groups)
-            for slot, pair in enumerate(pairs):
-                fork = fork_index(source, group, pair)
-                hit = (fork_child[fork] - group * rows == b) & (owner >= fork_block[fork])
-                kept = jnp.where(hit, fork_recv[away, slot].astype(F32), kept)
-        cache[b] = kept.astype(BF16)
 
     lane = lax.broadcasted_iota(jnp.int32, (grouping * rows, HD), 1)
     for j in range(KVH):
         heads = [j * grouping + i for i in range(grouping)]
-        grouped = jnp.concatenate([query[:, h * HD : (h + 1) * HD] for h in heads], axis=0)
-        keys = cache[:, :, j * HD : (j + 1) * HD].reshape(rows * positions_dev, HD)
-        values = cache[:, :, key_width + j * HD : key_width + (j + 1) * HD].reshape(
-            rows * positions_dev, HD
-        )
-        scores = lax.dot_general(
-            grouped, keys, (((1,), (1,)), ((), ())), preferred_element_type=F32
-        )
-        scores = scores * score_scale + bias
-        peak = jnp.max(scores, axis=1, keepdims=True)
-        weights = jnp.where(scores > 0.5 * HIDDEN_SCORE, jnp.exp(scores - peak), 0.0)
-        total = jnp.sum(weights, axis=1, keepdims=True)
-        part = jnp.dot(weights.astype(BF16), values, preferred_element_type=F32)
+        scores = own_scores[j]
+        fork_scores = raw_scores(j, head_rows(fork_recv, j * HD)) + fork_bias
+        peak = jnp.maximum(
+            jnp.max(scores, axis=1, keepdims=True), jnp.max(fork_scores, axis=1, keepdims=True)
+        )
+        total = jnp.zeros_like(peak)
+        part = jnp.zeros((grouping * rows, HD), F32)
+        for some, held in ((scores, kv_cache), (fork_scores, fork_recv)):
+            weights = jnp.where(some > 0.5 * HIDDEN_SCORE, jnp.exp(some - peak), 0.0)
+            total = total + jnp.sum(weights, axis=1, keepdims=True)
+            part = part + jnp.dot(
+                weights.astype(BF16),
+                head_rows(held, key_width + j * HD),
+                preferred_element_type=F32,
+            )
         peak_high = peak.astype(BF16).astype(F32)
         peak_mid = (peak - peak_high).astype(BF16).astype(F32)
         peak_low = peak - peak_high - peak_mid
@@ -238,11 +300,8 @@
 
     lax.fori_loop(1, owners, send_proj, 0)
     proj_recv[owner] = proj_send[owner]
-    if slice_residual:
-        start = pl.multiple_of(owner * columns, 128)
-        own_residual = residual[:, pl.ds(start, columns)].astype(F32)
-    else:
-        own_residual = residual[...].astype(F32)
+    small[7].wait()
+    own_residual = residual[...].astype(F32)
     take(proj_recv.at[pl.ds(0, owners - 1)], proj_sem.at[1])
     projected = jnp.sum(proj_recv[...].astype(F32), axis=0)
     attn_out[...] = projected.astype(BF16)
@@ -272,9 +331,17 @@
 
     lax.fori_loop(0, owners, send_stream, 0)
     tokens = groups * rows
-    lane_ids = route_ids[...]
+    small[8].wait()
+    small[9].wait()
     gates = jnp.sum(
-        jnp.where(lane_ids == owner, route_weights[...], 0.0), axis=1, keepdims=True
+        jnp.where(route_ids[...] == owner, route_weights[...], 0.0), axis=0, keepdims=True
+    )
+    square = (tokens, tokens)
+    diagonal = lax.broadcasted_iota(jnp.int32, square, 0) == lax.broadcasted_iota(
+        jnp.int32, square, 1
+    )
+    gates = jnp.sum(
+        jnp.where(diagonal, jnp.broadcast_to(gates, square), 0.0), axis=1, keepdims=True
     )
     loads[1].wait()
     loads[2].wait()
@@ -379,18 +446,26 @@
         )
     fork_rows = (math.isqrt(fork_parent.shape[0]) // groups) ** 2
     fork_shape = (groups, fork_rows) + kv_cache.shape[1:]
-    smem = pl.BlockSpec(memory_space=pltpu.SMEM)
     vmem = pl.BlockSpec(memory_space=pltpu.VMEM)
-    anywhere = pl.BlockSpec(memory_space=pl.ANY)
+    far = pl.BlockSpec(memory_space=pltpu.HBM)
     dma = pltpu.SemaphoreType.DMA
     block = jax.ShapeDtypeStruct((rows, columns), BF16)
     return pl.pallas_call(
         functools.partial(layer, groups, owners, slice_residual),
         out_shape=(block, block),
-        in_specs=[smem] * 4 + [vmem] * 6 + [anywhere] * 4,
+        in_specs=[far] * 14,
         out_specs=(vmem, vmem),
         scratch_shapes=[
+            pltpu.SMEM(lengths.shape, jnp.int32),
+            pltpu.SMEM(fork_parent.shape, jnp.int32),
+            pltpu.SMEM(fork_child.shape, jnp.int32),
+            pltpu.SMEM(fork_block.shape, jnp.int32),
+            pltpu.VMEM(query.shape, BF16),
+            pltpu.VMEM(new_kv.shape, BF16),
             pltpu.VMEM(kv_cache.shape, BF16),
+            pltpu.VMEM((rows, columns), BF16),
+            pltpu.VMEM(route_ids.shape[::-1], jnp.int32),
+            pltpu.VMEM(route_weights.shape[::-1], F32),
             pltpu.VMEM(out_weight.shape, BF16),
             pltpu.VMEM(w_gate.shape[1:], BF16),
             pltpu.VMEM(w_up.shape[1:], BF16),
@@ -405,6 +480,7 @@
             pltpu.VMEM((devices, rows, columns), BF16),
             pltpu.VMEM((devices, rows, columns), BF16),
             dma((4,)),
+            dma((10,)),
             dma((groups,)),
             dma((groups,)),
             dma((2,)),
@@ -414,7 +490,7 @@
             dma((2,)),
         ],
         compiler_params=pltpu.CompilerParams(
-            collective_id=0, has_side_effects=True, vmem_limit_bytes=48 * 1024 * 1024
+            collective_id=0, has_side_effects=True, vmem_limit_bytes=64 * 1024 * 1024
         ),
     )(
         lengths,
@@ -425,8 +501,8 @@
         new_kv,
         kv_cache,
         residual,
-        route_ids,
-        route_weights,
+        route_ids.T,
+        route_weights.T,
         out_weight,
         w_gate,
         w_up,

time: 50.9 us -> 41 us (0.81)
  local copies, waits for them, and re-layouts: 12.3 us -> 2.59 us
    unnamed x24 -> x2, local copies, waits for them, and re-layouts: 12.3 us -> 2.59 us
where the time goes in v2:
time: 41 us; the launch traced here: 40.5 us
  Pallas kernels  37.3 us (91%)
  local copies, waits for them, and re-layouts  2.59 us (6%)
  between operations  0.64 us (2%)
    pallas_call x1, Pallas kernels, shards(): pl.pallas_call(functools.partial(layer, groups, owners, slice_residual),...  37.3 us
    unnamed x2, local copies, waits for them, and re-layouts  2.59 us

profile of v2, /device:TPU:0, one launch (start us, length us, event | category | flops | bytes accessed | tf_op | source)
XLA Modules:
  0.0 40.5 jit_solution(9226562065567969989)
XLA Ops:
  0.6 37.3 %shard_map.149 = (bf16[16,256]{1,0:T(8,128)(2,1)}, bf16[16,256]{1,0:T(8,128)(2,1)}) custom-call(s32[16]{0:T(128)} %lengths_in.1, s32[4]{0:T(128)} %fork_parent_in.1, s32[4]{0:T(128)} %fork_child_in.1, s32[4]{0:T(128)} %fork_block_in.1, bf16[16,2048]{1,0:T(8,128)(2,1)} %query_in.1, bf16[16,1024]{1,0:T(8,128)(2,1)} %new_kv_in.1, ...), custom_call_target="tpu_custom_call" | custom-call | tf_op jit(solution)/shard_map/pallas_call | solution.py:453
  37.9 1.3 %copy.18 = bf16[16,256]{1,0:T(8,128)(2,1)} copy(bf16[16,256]{1,0:T(8,128)(2,1)} %get-tuple-element.4) | data formatting | bytes 16384
  39.2 1.3 %copy.19 = bf16[16,256]{1,0:T(8,128)(2,1)} copy(bf16[16,256]{1,0:T(8,128)(2,1)} %get-tuple-element.5) | data formatting | bytes 16384

commit v3 on v2

--- a/solution.py
+++ b/solution.py
@@ -58,6 +58,8 @@
     proj_recv,
     stream,
     mix_send,
+    mix_pair,
+    mix_sum,
     mix_recv,
     load_sem,
     small_sem,
@@ -65,13 +67,14 @@
     fork_recv_sem,
     part_sem,
     proj_sem,
-    stream_send_sem,
+    stream_sem,
     stream_recv_sem,
+    relay_sem,
+    pair_sem,
     mix_sem,
 ):
     group = lax.axis_index("dp")
     owner = lax.axis_index("expert")
-    devices = groups * owners
     rows = query.shape[0]
     positions_dev = kv_cache.shape[1]
     key_width = KVH * HD
@@ -82,16 +85,28 @@
     held_groups = fork_groups // groups
     pairs = [(i, k) for i in range(held_groups) for k in range(held_groups)]
 
+    half = owners // 2
+    core = lax.rem(owner, 2)
+    chip = owner // 2
+    sibling = owner + 1 - 2 * core
+
+    def same_core(step):
+        return 2 * lax.rem(chip + step, half) + core
+
     barrier = pltpu.get_barrier_semaphore()
 
-    def greet(step, carry):
-        place = lax.rem(group * owners + owner + step, devices)
+    def greet(to_group, to_owner):
         pl.semaphore_signal(
-            barrier,
-            inc=1,
-            device_id=(place // owners, lax.rem(place, owners)),
-            device_id_type=MESH,
-        )
+            barrier, inc=1, device_id=(to_group, to_owner), device_id_type=MESH
+        )
+
+    def greet_group(step, carry):
+        greet(group, lax.rem(owner + step, owners))
+        return carry
+
+    def greet_others(step, carry):
+        for away in range(1, groups):
+            greet(lax.rem(group + away, groups), same_core(step))
         return carry
 
     start = pl.multiple_of(owner * columns, columns)
@@ -115,7 +130,8 @@
     ]
     for load in small:
         load.start()
-    lax.fori_loop(1, devices, greet, 0)
+    lax.fori_loop(1, owners, greet_group, 0)
+    lax.fori_loop(0, half, greet_others, 0)
 
     loads = [
         pltpu.make_async_copy(out_weight, out_held, load_sem.at[0]),
@@ -189,7 +205,7 @@
         child_at = jnp.where(fork_at == i, child, child_at)
     fork_bias = bias_of(seen & (child_at == row_at))
 
-    pl.semaphore_wait(barrier, devices - 1)
+    pl.semaphore_wait(barrier, owners - 1 + (groups - 1) * half)
     for away in range(1, groups):
         target = lax.rem(group + away, groups)
         send(
@@ -306,21 +322,19 @@
     projected = jnp.sum(proj_recv[...].astype(F32), axis=0)
     attn_out[...] = projected.astype(BF16)
     own_rows = pl.ds(pl.multiple_of(group * rows, rows), rows)
-    stream[owner, own_rows, :] = (own_residual + projected).astype(BF16)
+    stream[core, chip, own_rows, :] = (own_residual + projected).astype(BF16)
 
     def send_stream(step, carry):
-        target = lax.rem(owner + step, owners)
         for away in range(groups):
-            to_group = lax.rem(group + away, groups)
 
             def go():
                 send(
-                    stream.at[owner, own_rows],
-                    stream.at[owner, own_rows],
-                    stream_send_sem,
-                    stream_recv_sem.at[owner, group],
-                    to_group,
-                    target,
+                    stream.at[core, chip, own_rows],
+                    stream.at[core, chip, own_rows],
+                    stream_sem.at[0],
+                    stream_recv_sem.at[chip, group],
+                    lax.rem(group + away, groups),
+                    same_core(step),
                 )
 
             if away == 0:
@@ -329,7 +343,7 @@
                 go()
         return carry
 
-    lax.fori_loop(0, owners, send_stream, 0)
+    lax.fori_loop(0, half, send_stream, 0)
     tokens = groups * rows
     small[8].wait()
     small[9].wait()
@@ -345,75 +359,120 @@
     )
     loads[1].wait()
     loads[2].wait()
-    inner = tile // columns
+    chunks = width // tile
+    inner = tile // columns // 2
     units = gate_held.shape[1]
 
-    def expand(step, state):
+    def expand(side, chunk, state):
         gate_sum, up_sum, squares = state
-        chunk = lax.rem(owner // inner + step, owners // inner)
         for i in range(inner):
-            source = chunk * inner + i
+            block = chunk * inner + i
+            x = stream[side, block]
+            depth = pl.ds(pl.multiple_of((2 * block + side) * columns, columns), columns)
+            gate_sum = gate_sum + jnp.dot(x, gate_held[depth, :], preferred_element_type=F32)
+            up_sum = up_sum + jnp.dot(x, up_held[depth, :], preferred_element_type=F32)
+            wide = x.astype(F32)
+            squares = squares + jnp.sum(wide * wide, axis=1, keepdims=True)
+        return gate_sum, up_sum, squares
+
+    def chunk_at(step):
+        return lax.rem(chip // inner + step, chunks)
+
+    def expand_arrived(step, state):
+        chunk = chunk_at(step)
+        for i in range(inner):
+            block = chunk * inner + i
             for g in range(groups):
 
-                @pl.when((source != owner) | (g != group))
+                @pl.when((block != chip) | (g != group))
                 def _():
                     take(
-                        stream.at[source, pl.ds(g * rows, rows)], stream_recv_sem.at[source, g]
+                        stream.at[core, block, pl.ds(g * rows, rows)],
+                        stream_recv_sem.at[block, g],
                     )
 
-        x = jnp.concatenate([stream[chunk * inner + i] for i in range(inner)], axis=1)
-        depth = pl.ds(pl.multiple_of(chunk * tile, tile), tile)
-        gate_sum = gate_sum + jnp.dot(x, gate_held[depth, :], preferred_element_type=F32)
-        up_sum = up_sum + jnp.dot(x, up_held[depth, :], preferred_element_type=F32)
-        wide = x.astype(F32)
-        return gate_sum, up_sum, squares + jnp.sum(wide * wide, axis=1, keepdims=True)
+        relayed = stream.at[core, pl.ds(chunk * inner, inner)]
+        send(relayed, relayed, stream_sem.at[1], relay_sem.at[chunk], group, sibling)
+        return expand(core, chunk, state)
+
+    def expand_relayed(step, state):
+        chunk = chunk_at(step)
+        take(stream.at[1 - core, pl.ds(chunk * inner, inner)], relay_sem.at[chunk])
+        return expand(1 - core, chunk, state)
 
     zero = jnp.zeros((tokens, units), F32)
-    gate_sum, up_sum, squares = lax.fori_loop(
-        0, owners // inner, expand, (zero, zero, jnp.zeros((tokens, 1), F32))
-    )
+    state = (zero, zero, jnp.zeros((tokens, 1), F32))
+    state = lax.fori_loop(0, chunks, expand_arrived, state)
+    gate_sum, up_sum, squares = lax.fori_loop(0, chunks, expand_relayed, state)
     inverse = lax.rsqrt(squares / width + 1e-06)
     gate_sum = gate_sum * inverse
     hidden = (gate_sum / (1.0 + jnp.exp(-gate_sum)) * (up_sum * inverse)).astype(BF16)
 
     loads[3].wait()
-    place = group * owners + owner
-
-    def contract(step, carry):
-        chunk = lax.rem(owner // inner + step, owners // inner)
+    place = group * half + chip
+
+    def contract(step):
+        chunk = chunk_at(step)
         span = pl.ds(pl.multiple_of(chunk * tile, tile), tile)
         terms = jnp.dot(hidden, down_held[:, span], preferred_element_type=F32)
         terms = (terms * gates).astype(BF16)
         for i in range(inner):
-            target = chunk * inner + i
+            for side in range(2):
+                at = (2 * i + side) * columns
+                for g in range(groups):
+                    mix_send[side, chunk * inner + i, g] = terms[
+                        g * rows : (g + 1) * rows, at : at + columns
+                    ]
+        some = pl.ds(chunk * inner, inner)
+        send(
+            mix_send.at[1 - core, some],
+            mix_pair.at[some],
+            mix_sem.at[0],
+            pair_sem.at[chunk],
+            group,
+            sibling,
+        )
+
+    def spread_sums(step):
+        chunk = chunk_at(step)
+        some = pl.ds(chunk * inner, inner)
+        take(mix_pair.at[some], pair_sem.at[chunk])
+        mix_sum[some] = (mix_send[core, some].astype(F32) + mix_pair[some].astype(F32)).astype(
+            BF16
+        )
+        for i in range(inner):
+            block = chunk * inner + i
             for g in range(groups):
-                slot = g * owners + target
-                mix_send[slot] = terms[g * rows : (g + 1) * rows, i * columns : (i + 1) * columns]
-
-                @pl.when(slot != place)
+
+                @pl.when((block != chip) | (g != group))
                 def _():
                     send(
-                        mix_send.at[slot],
+                        mix_sum.at[block, g],
                         mix_recv.at[place],
-                        mix_sem.at[0],
                         mix_sem.at[1],
+                        mix_sem.at[2],
                         g,
-                        target,
+                        2 * block + core,
                     )
 
-        return carry
-
-    lax.fori_loop(0, owners // inner, contract, 0)
-    mix_recv[place] = mix_send[place]
-    take(mix_recv.at[pl.ds(0, devices - 1)], mix_sem.at[1])
+    for step in range(chunks):
+        contract(step)
+        if step > 0:
+            spread_sums(step - 1)
+    spread_sums(chunks - 1)
+    mix_recv[place] = mix_sum[chip, group]
+    others = pl.ds(0, half * groups - 1)
+    take(mix_recv.at[others], mix_sem.at[2])
     mix_out[...] = jnp.sum(mix_recv[...].astype(F32), axis=0).astype(BF16)
 
     for away in range(1, groups):
         take(fork_send.at[away], fork_send_sem.at[away])
     take(part_send.at[pl.ds(0, owners - 1)], part_sem.at[0])
     take(proj_send.at[pl.ds(0, owners - 1)], proj_sem.at[0])
-    take(mix_send.at[pl.ds(0, devices - 1)], stream_send_sem)
-    take(mix_send.at[pl.ds(0, devices - 1)], mix_sem.at[0])
+    take(mix_recv.at[others], stream_sem.at[0])
+    take(stream.at[0], stream_sem.at[1])
+    take(mix_pair, mix_sem.at[0])
+    take(mix_recv.at[others], mix_sem.at[1])
 
 
 def shards(
@@ -434,11 +493,12 @@
 ):
     groups = lax.axis_size("dp")
     owners = lax.axis_size("expert")
-    devices = groups * owners
+    half = owners // 2
     rows, positions_dev, _ = kv_cache.shape
     heads = query.shape[1] // HD
     width = residual.shape[1]
     columns = width // owners
+    chunks = width // max(columns, 1024)
     slice_residual = columns % 128 == 0
     if not slice_residual:
         residual = lax.dynamic_slice_in_dim(
@@ -476,18 +536,22 @@
             pltpu.VMEM((owners, rows, 2 * HD), BF16),
             pltpu.VMEM((owners, rows, columns), BF16),
             pltpu.VMEM((owners, rows, columns), BF16),
-            pltpu.VMEM((owners, groups * rows, columns), BF16),
-            pltpu.VMEM((devices, rows, columns), BF16),
-            pltpu.VMEM((devices, rows, columns), BF16),
+            pltpu.VMEM((2, half, groups * rows, columns), BF16),
+            pltpu.VMEM((2, half, groups, rows, columns), BF16),
+            pltpu.VMEM((half, groups, rows, columns), BF16),
+            pltpu.VMEM((half, groups, rows, columns), BF16),
+            pltpu.VMEM((half * groups, rows, columns), BF16),
             dma((4,)),
             dma((10,)),
             dma((groups,)),
             dma((groups,)),
             dma((2,)),
             dma((2,)),
-            dma,
-            dma((owners, groups)),
             dma((2,)),
+            dma((half, groups)),
+            dma((chunks,)),
+            dma((chunks,)),
+            dma((3,)),
         ],
         compiler_params=pltpu.CompilerParams(
             collective_id=0, has_side_effects=True, vmem_limit_bytes=64 * 1024 * 1024

time: 41 us -> 39.6 us (0.966)
  Pallas kernels: 37.3 us -> 36.1 us
    pallas_call x1, Pallas kernels: 37.3 us -> 36.1 us  [shards(): pl.pallas_call(functools.partial(layer, groups, owners, slice_residual),...]
where the time goes in v3:
time: 39.6 us; the launch traced here: 39.3 us
  Pallas kernels  36.1 us (91%)
  local copies, waits for them, and re-layouts  2.59 us (7%)
  between operations  0.64 us (2%)
    pallas_call x1, Pallas kernels, shards(): pl.pallas_call(functools.partial(layer, groups, owners, slice_residual),...  36.1 us
    unnamed x2, local copies, waits for them, and re-layouts  2.59 us

profile of v3, /device:TPU:0, one launch (start us, length us, event | category | flops | bytes accessed | tf_op | source)
XLA Modules:
  0.0 39.3 jit_solution(15963299929814084930)
XLA Ops:
  0.6 36.1 %shard_map.149 = (bf16[16,256]{1,0:T(8,128)(2,1)}, bf16[16,256]{1,0:T(8,128)(2,1)}) custom-call(s32[16]{0:T(128)} %lengths_in.1, s32[4]{0:T(128)} %fork_parent_in.1, s32[4]{0:T(128)} %fork_child_in.1, s32[4]{0:T(128)} %fork_block_in.1, bf16[16,2048]{1,0:T(8,128)(2,1)} %query_in.1, bf16[16,1024]{1,0:T(8,128)(2,1)} %new_kv_in.1, ...), custom_call_target="tpu_custom_call" | custom-call | tf_op jit(solution)/shard_map/pallas_call | solution.py:513
  36.7 1.3 %copy.18 = bf16[16,256]{1,0:T(8,128)(2,1)} copy(bf16[16,256]{1,0:T(8,128)(2,1)} %get-tuple-element.4) | data formatting | bytes 16384
  38.0 1.3 %copy.19 = bf16[16,256]{1,0:T(8,128)(2,1)} copy(bf16[16,256]{1,0:T(8,128)(2,1)} %get-tuple-element.5) | data formatting | bytes 16384

commit v4 on v3

--- a/solution.py
+++ b/solution.py
@@ -34,8 +34,7 @@
     w_gate,
     w_up,
     w_down,
-    attn_out,
-    mix_out,
+    outs,
     lengths,
     fork_parent,
     fork_child,
@@ -320,7 +319,7 @@
     own_residual = residual[...].astype(F32)
     take(proj_recv.at[pl.ds(0, owners - 1)], proj_sem.at[1])
     projected = jnp.sum(proj_recv[...].astype(F32), axis=0)
-    attn_out[...] = projected.astype(BF16)
+    outs[0] = projected.astype(BF16)
     own_rows = pl.ds(pl.multiple_of(group * rows, rows), rows)
     stream[core, chip, own_rows, :] = (own_residual + projected).astype(BF16)
 
@@ -395,15 +394,14 @@
         send(relayed, relayed, stream_sem.at[1], relay_sem.at[chunk], group, sibling)
         return expand(core, chunk, state)
 
-    def expand_relayed(step, state):
-        chunk = chunk_at(step)
-        take(stream.at[1 - core, pl.ds(chunk * inner, inner)], relay_sem.at[chunk])
-        return expand(1 - core, chunk, state)
-
     zero = jnp.zeros((tokens, units), F32)
     state = (zero, zero, jnp.zeros((tokens, 1), F32))
     state = lax.fori_loop(0, chunks, expand_arrived, state)
-    gate_sum, up_sum, squares = lax.fori_loop(0, chunks, expand_relayed, state)
+    for chunk in range(chunks):
+        take(stream.at[1 - core, pl.ds(chunk * inner, inner)], relay_sem.at[chunk])
+    for chunk in range(chunks):
+        state = expand(1 - core, chunk, state)
+    gate_sum, up_sum, squares = state
     inverse = lax.rsqrt(squares / width + 1e-06)
     gate_sum = gate_sum * inverse
     hidden = (gate_sum / (1.0 + jnp.exp(-gate_sum)) * (up_sum * inverse)).astype(BF16)
@@ -463,7 +461,7 @@
     mix_recv[place] = mix_sum[chip, group]
     others = pl.ds(0, half * groups - 1)
     take(mix_recv.at[others], mix_sem.at[2])
-    mix_out[...] = jnp.sum(mix_recv[...].astype(F32), axis=0).astype(BF16)
+    outs[1] = jnp.sum(mix_recv[...].astype(F32), axis=0).astype(BF16)
 
     for away in range(1, groups):
         take(fork_send.at[away], fork_send_sem.at[away])
@@ -509,12 +507,11 @@
     vmem = pl.BlockSpec(memory_space=pltpu.VMEM)
     far = pl.BlockSpec(memory_space=pltpu.HBM)
     dma = pltpu.SemaphoreType.DMA
-    block = jax.ShapeDtypeStruct((rows, columns), BF16)
-    return pl.pallas_call(
+    both = pl.pallas_call(
         functools.partial(layer, groups, owners, slice_residual),
-        out_shape=(block, block),
+        out_shape=jax.ShapeDtypeStruct((2, rows, columns), BF16),
         in_specs=[far] * 14,
-        out_specs=(vmem, vmem),
+        out_specs=vmem,
         scratch_shapes=[
             pltpu.SMEM(lengths.shape, jnp.int32),
             pltpu.SMEM(fork_parent.shape, jnp.int32),
@@ -572,6 +569,7 @@
         w_up,
         w_down,
     )
+    return both[0], both[1]
 
 
 def solution(mesh):

time: 39.6 us -> 38.2 us (0.965)
  local copies, waits for them, and re-layouts: 2.59 us -> 1.32 us
    unnamed x2 -> x0, local copies, waits for them, and re-layouts: 2.59 us -> none
    squeeze x0 -> x1, local copies, waits for them, and re-layouts: none -> 1.32 us  [shards(): return (both[0], both[1])]
where the time goes in v4:
time: 38.2 us; the launch traced here: 38 us
  Pallas kernels  36 us (94%)
  local copies, waits for them, and re-layouts  1.32 us (3%)
  between operations  0.64 us (2%)
    pallas_call x1, Pallas kernels, shards(): pl.pallas_call(functools.partial(layer, groups, owners, slice_residual),...  36 us
    squeeze x1, local copies, waits for them, and re-layouts, shards(): return (both[0], both[1])  1.32 us

profile of v4, /device:TPU:0, one launch (start us, length us, event | category | flops | bytes accessed | tf_op | source)
XLA Modules:
  0.0 38.0 jit_solution(5819642057154595122)
XLA Ops:
  0.6 36.0 %shard_map.149 = bf16[2,16,256]{2,1,0:T(8,128)(2,1)} custom-call(s32[16]{0:T(128)} %lengths_in.1, s32[4]{0:T(128)} %fork_parent_in.1, s32[4]{0:T(128)} %fork_child_in.1, s32[4]{0:T(128)} %fork_block_in.1, bf16[16,2048]{1,0:T(8,128)(2,1)} %query_in.1, bf16[16,1024]{1,0:T(8,128)(2,1)} %new_kv_in.1, bf16[16,16,1024]{2,1,0:T(8,128)(2,1)} %kv_cache_in.1, ...), custom_call_target="tpu_custom_call" | custom-call | tf_op jit(solution)/shard_map/pallas_call | solution.py:510
  36.7 1.3 %slice_bitcast_fusion = (bf16[16,256]{1,0:T(8,128)(2,1)}, bf16[16,256]{1,0:T(8,128)(2,1)}) fusion(bf16[2,16,256]{2,1,0:T(8,128)(2,1)} %shard_map.149), kind=kLoop, calls=%fused_computation | loop fusion | bytes 32768 | tf_op jit(solution)/shard_map/squeeze | solution.py:572

commit v5 on v4

--- a/solution.py
+++ b/solution.py
@@ -299,21 +299,25 @@
     loads[0].wait()
     tile = max(columns, 1024)
     blocks = tile // columns
-    for k in range(width // tile):
-        terms = jnp.dot(
-            attended, out_held[:, k * tile : (k + 1) * tile], preferred_element_type=F32
-        ).astype(BF16)
+    for step in range(width // tile):
+        chunk = lax.rem(owner // blocks + step + 1, width // tile)
+        span = pl.ds(pl.multiple_of(chunk * tile, tile), tile)
+        terms = jnp.dot(attended, out_held[:, span], preferred_element_type=F32).astype(BF16)
         for i in range(blocks):
-            proj_send[k * blocks + i] = terms[:, i * columns : (i + 1) * columns]
-
-    def send_proj(step, carry):
-        target = lax.rem(owner + step, owners)
-        send(
-            proj_send.at[target], proj_recv.at[owner], proj_sem.at[0], proj_sem.at[1], group, target
-        )
-        return carry
-
-    lax.fori_loop(1, owners, send_proj, 0)
+            target = chunk * blocks + i
+            proj_send[target] = terms[:, i * columns : (i + 1) * columns]
+
+            @pl.when(target != owner)
+            def _():
+                send(
+                    proj_send.at[target],
+                    proj_recv.at[owner],
+                    proj_sem.at[0],
+                    proj_sem.at[1],
+                    group,
+                    target,
+                )
+
     proj_recv[owner] = proj_send[owner]
     small[7].wait()
     own_residual = residual[...].astype(F32)
@@ -410,7 +414,7 @@
     place = group * half + chip
 
     def contract(step):
-        chunk = chunk_at(step)
+        chunk = chunk_at(step + 1)
         span = pl.ds(pl.multiple_of(chunk * tile, tile), tile)
         terms = jnp.dot(hidden, down_held[:, span], preferred_element_type=F32)
         terms = (terms * gates).astype(BF16)
@@ -432,7 +436,7 @@
         )
 
     def spread_sums(step):
-        chunk = chunk_at(step)
+        chunk = chunk_at(step + 1)
         some = pl.ds(chunk * inner, inner)
         take(mix_pair.at[some], pair_sem.at[chunk])
         mix_sum[some] = (mix_send[core, some].astype(F32) + mix_pair[some].astype(F32)).astype(

time: 38.2 us -> 37.7 us (0.987)
  Pallas kernels: 36 us -> 35.6 us
    pallas_call x1, Pallas kernels: 36 us -> 35.6 us  [shards(): pl.pallas_call(functools.partial(layer, groups, owners, slice_residual),...]
where the time goes in v5:
time: 37.7 us; the launch traced here: 37.5 us
  Pallas kernels  35.6 us (94%)
  local copies, waits for them, and re-layouts  1.32 us (4%)
  between operations  0.64 us (2%)
    pallas_call x1, Pallas kernels, shards(): pl.pallas_call(functools.partial(layer, groups, owners, slice_residual),...  35.6 us
    squeeze x1, local copies, waits for them, and re-layouts, shards(): return (both[0], both[1])  1.32 us

profile of v5, /device:TPU:0, one launch (start us, length us, event | category | flops | bytes accessed | tf_op | source)
XLA Modules:
  0.0 37.5 jit_solution(8952422411471741674)
XLA Ops:
  0.6 35.6 %shard_map.149 = bf16[2,16,256]{2,1,0:T(8,128)(2,1)} custom-call(s32[16]{0:T(128)} %lengths_in.1, s32[4]{0:T(128)} %fork_parent_in.1, s32[4]{0:T(128)} %fork_child_in.1, s32[4]{0:T(128)} %fork_block_in.1, bf16[16,2048]{1,0:T(8,128)(2,1)} %query_in.1, bf16[16,1024]{1,0:T(8,128)(2,1)} %new_kv_in.1, bf16[16,16,1024]{2,1,0:T(8,128)(2,1)} %kv_cache_in.1, ...), custom_call_target="tpu_custom_call" | custom-call | tf_op jit(solution)/shard_map/pallas_call | solution.py:514
  36.2 1.3 %slice_bitcast_fusion = (bf16[16,256]{1,0:T(8,128)(2,1)}, bf16[16,256]{1,0:T(8,128)(2,1)}) fusion(bf16[2,16,256]{2,1,0:T(8,128)(2,1)} %shard_map.149), kind=kLoop, calls=%fused_computation | loop fusion | bytes 32768 | tf_op jit(solution)/shard_map/squeeze | solution.py:576
